TPU v7x, 512 devices: a whole 4x4x16 slice. The times are simulated.
512 devices in a mesh: tensor: 4 (over y), shard: 32 (over x_hi, z), replica: 4 (over x_lo, core).
Axes of the slice: x: 4 (x_hi: 2, x_lo: 2; x = x_hi * 2 + x_lo), y: 4, z: 16, core: 2. Of those that a mesh axis runs over, the one named last changes fastest.
Arguments:
- activations: bfloat16 [32768, 8192], P(('shard', 'replica'), 'tensor'), may hold values from -6 to 6
- queries: bfloat16 [32768, 4096], P(('shard', 'replica'), 'tensor'), may hold values from -48 to 48
- key_vectors: bfloat16 [32768, 512], P(('shard', 'replica'), 'tensor'), may hold values from -4 to 4
- grad_output: bfloat16 [32768, 4096], P(('shard', 'replica'), 'tensor'), may hold values from -6 to 6
- segment_ids: int32 [32768], P(('shard', 'replica')), may hold values from 0 to 511, never falling along the last dimension, each value on 1 to 128 neighbouring positions
- value_weight: bfloat16 [8192, 512], P('shard', 'tensor'), may hold values from -0.0625 to 0.0625
- master: float32 [8192, 512], P('shard', 'tensor'), may hold values from -3 to 3
- first_moment: float32 [8192, 512], P('shard', 'tensor'), may hold values from -3 to 3
- second_moment: float32 [8192, 512], P('shard', 'tensor'), may hold values from 0.01 to 1
Outputs:
- grad_queries: bfloat16 [32768, 4096], P(('shard', 'replica'), 'tensor')
- grad_keys: bfloat16 [32768, 512], P(('shard', 'replica'), 'tensor')
- gradient: float32 [8192, 512], P('shard', 'tensor')
- new_master: float32 [8192, 512], P('shard', 'tensor')
- new_first: float32 [8192, 512], P('shard', 'tensor')
- new_second: float32 [8192, 512], P('shard', 'tensor')
Inputs may be any that keep to these rules, and one draw needn't show every extreme that they name: `segment_ids`: never falls along the tokens; each document spans at most half of 256 positions, and one spans exactly that many.
All inputs are finite; a program needn't handle non-finite values.
Results may differ from a plain program's by a relative error of at most 0.025.
Values may be sent and summed in bfloat16 or wider, within the bound.
A program may use at most 64 MiB of HBM per device.

v0:
```python
import math

import jax
import jax.numpy as jnp
from jax import lax
from jax.sharding import PartitionSpec as P

STEP = 10


BETA_FIRST = 0.9
BETA_SECOND = 0.95
LEARN_RATE = 0.001
WEIGHT_DECAY = 0.1
EPSILON = 1e-08


def block_grads(
    query_block, key_rows, values, grad_block, seg_block, all_segments, pos_block, positions, factor
):
    scores = (
        jnp.einsum("bgd,td->gbt", query_block, key_rows, preferred_element_type=jnp.float32)
        * factor
    )
    allowed = (seg_block[:, None] == all_segments[None, :]) & (
        positions[None, :] <= pos_block[:, None]
    )
    scores = jnp.where(allowed[None], scores, -1e30)
    row_max = jnp.max(scores, axis=2, keepdims=True)
    powered = jnp.exp(scores - row_max)
    weights = powered / jnp.sum(powered, axis=2, keepdims=True)
    rounded = weights.astype(jnp.bfloat16)
    outputs = jnp.einsum("gbt,td->bgd", rounded, values, preferred_element_type=jnp.float32)
    row_dot = jnp.sum(grad_block.astype(jnp.float32) * outputs, axis=2)
    grad_weights = jnp.einsum("bgd,td->gbt", grad_block, values, preferred_element_type=jnp.float32)
    grad_scores = (weights * (grad_weights - jnp.transpose(row_dot)[:, :, None]) * factor).astype(
        jnp.bfloat16
    )
    query_grad = jnp.einsum(
        "gbt,td->bgd", grad_scores, key_rows, preferred_element_type=jnp.float32
    ).astype(jnp.bfloat16)
    key_grad = jnp.einsum(
        "gbt,bgd->td", grad_scores, query_block, preferred_element_type=jnp.float32
    )
    value_grad = jnp.einsum("gbt,bgd->td", rounded, grad_block, preferred_element_type=jnp.float32)
    return (query_grad, key_grad, value_grad)


def per_device(
    activations,
    queries,
    key_vectors,
    grad_output,
    segment_ids,
    value_weight,
    master,
    first_moment,
    second_moment,
):
    length = activations.shape[0]
    head_size = value_weight.shape[1]
    per_group = queries.shape[1] // head_size
    gathered = lax.all_gather(activations, "tensor", axis=1, tiled=True)
    columns = gathered
    values = jnp.dot(
        columns,
        lax.all_gather(value_weight, "shard", axis=0, tiled=True),
        preferred_element_type=jnp.float32,
    ).astype(jnp.bfloat16)
    factor = 1.0 / math.sqrt(head_size)
    query_heads = queries.reshape(length, per_group, head_size)
    grad_heads = grad_output.reshape(length, per_group, head_size)
    positions = jnp.arange(length, dtype=jnp.int32)
    query_grad, key_grad, value_grad = block_grads(
        query_heads,
        key_vectors,
        values,
        grad_heads,
        segment_ids,
        segment_ids,
        positions,
        positions,
        factor,
    )
    grad_queries = query_grad.reshape(length, per_group * head_size)
    grad_keys = key_grad.astype(jnp.bfloat16)
    value_low = value_grad.astype(jnp.bfloat16)
    shard_count = lax.axis_size("shard")
    replica_count = lax.axis_size("replica")
    columns = gathered
    term = lax.dot_general(
        columns, value_low, (((0,), (0,)), ((), ())), preferred_element_type=jnp.float32
    )
    shard_part = lax.psum_scatter(
        term.astype(jnp.bfloat16).astype(jnp.float32).astype(jnp.bfloat16),
        "shard",
        scatter_dimension=0,
        tiled=True,
    )
    summed = lax.psum(shard_part, "replica").astype(jnp.float32)
    gradient = summed / (shard_count * replica_count)
    new_first = BETA_FIRST * first_moment + (1.0 - BETA_FIRST) * gradient
    new_second = BETA_SECOND * second_moment + (1.0 - BETA_SECOND) * gradient * gradient
    corrected = (
        new_first
        / (1.0 - BETA_FIRST**STEP)
        / (jnp.sqrt(new_second / (1.0 - BETA_SECOND**STEP)) + EPSILON)
    )
    new_master = master - LEARN_RATE * (corrected + WEIGHT_DECAY * master)
    return (grad_queries, grad_keys, gradient, new_master, new_first, new_second)


def solution(mesh):
    placed = (
        P(("shard", "replica"), "tensor"),
        P(("shard", "replica"), "tensor"),
        P(("shard", "replica"), "tensor"),
        P(("shard", "replica"), "tensor"),
        P(("shard", "replica")),
        P("shard", "tensor"),
        P("shard", "tensor"),
        P("shard", "tensor"),
        P("shard", "tensor"),
    )
    return jax.shard_map(
        per_device,
        mesh=mesh,
        in_specs=placed,
        out_specs=(
            P(("shard", "replica"), "tensor"),
            P(("shard", "replica"), "tensor"),
            P("shard", "tensor"),
            P("shard", "tensor"),
            P("shard", "tensor"),
            P("shard", "tensor"),
        ),
        check_vma=False,
    )
```

profile of v0, /device:TPU:1, one launch (start us, length us, event | category | flops | bytes accessed | tf_op | source)
XLA Modules:
  0.0 932.4 jit_solution(12041913660956830554)
XLA Ops:
  7.2 0.0 copy-start
  7.2 0.0 all-gather.3.cloned.1.call-start
  7.2 0.7 all-gather.3.cloned.1.call-update
  7.9 0.0 all-gather.5.cloned.1.call-start
  8.0 0.7 all-gather.5.cloned.1.call-update
  8.7 0.0 reduce-scatter.2.cloned.1.call-start
  8.7 1.2 copy.16
  10.0 0.1 fusion.20
  10.1 0.8 fusion.43
  11.0 60.4 %all-gather.3.cloned.1.call-done = bf16[256,8192]{1,0:T(8,128)(2,1)} async-done(((bf16[256,2048]{1,0:T(8,128)(2,1)}), bf16[256,8192]{1,0:T(8,128)(2,1)}) %all-gather.3.cloned.1.call-update) | async-done | bytes 4194320 | tf_op jit(solution)/shard_map/all_gather | solution.py:63
  71.4 5.2 fusion.1
  76.6 0.0 reduce-scatter.2.cloned.1.call-update
  76.7 0.0 all-reduce.2.cloned.1.call-start
  76.7 0.8 copy-done.1
  77.5 0.1 copy.26
  77.7 0.1 copy.23
  77.8 0.1 copy.24
  77.9 138.2 %all-gather.5.cloned.1.call-done = bf16[8192,128]{1,0:T(8,128)(2,1)} async-done(((bf16[256,128]{1,0:T(8,128)(2,1)}), bf16[8192,128]{1,0:T(8,128)(2,1)}) %all-gather.5.cloned.1.call-update) | async-done | bytes 2097168 | tf_op jit(solution)/shard_map/all_gather | solution.py:67
  216.1 4.2 fusion.10
  220.4 0.3 fusion.7
  220.7 0.5 fusion.4
  221.2 1.1 fusion.8
  222.3 637.2 %reduce-scatter.2.cloned.1.call-done = bf16[256,128]{0,1:T(8,128)(2,1)} async-done(((bf16[8192,128]{0,1:T(8,128)(2,1)}), bf16[256,128]{0,1:T(8,128)(2,1)}) %reduce-scatter.2.cloned.1.call-update) | async-done | bytes 65552 | tf_op jit(solution)/shard_map/reduce_scatter | solution.py:94
  859.5 0.0 all-reduce.2.cloned.1.call-update
  859.5 0.4 convolution_convert_fusion.1
  859.9 1.0 copy.27
  860.9 61.0 %all-reduce.2.cloned.1.call-done = bf16[256,128]{0,1:T(8,128)(2,1)} async-done(((bf16[256,128]{0,1:T(8,128)(2,1)}), bf16[256,128]{0,1:T(8,128)(2,1)}) %all-reduce.2.cloned.1.call-update) | async-done | bytes 65552 | tf_op jit(solution)/shard_map/psum | solution.py:100
  921.9 1.0 multiply_subtract_fusion
  922.9 0.8 copy.29
  923.6 0.8 copy.30
  924.4 0.8 copy.31
  925.1 0.8 copy.28
  (14 shorter events, 0.0 us)
Async XLA Ops:
  7.2 2.9 copy-start
  7.2 2.8 copy-start.5
  7.2 2.9 copy-start.4
  7.2 64.2 %all-gather.3.cloned.1.call-start = ((), (), s32[]{:S(2)}) async-start(), calls=%async_computation.1 | async-start | bytes 5242880 | tf_op jit(solution)/shard_map/all_gather | solution.py:63
  7.9 208.2 %all-gather.5.cloned.1.call-start = ((), (), s32[]{:S(2)}) async-start(), calls=%async_computation.2 | async-start | bytes 2162688 | tf_op jit(solution)/shard_map/all_gather | solution.py:67
  8.7 850.8 %reduce-scatter.2.cloned.1.call-start = ((), (), s32[]{:S(2)}) async-start(), calls=%async_computation.3 | async-start | bytes 2162688 | tf_op jit(solution)/shard_map/reduce_scatter | solution.py:94
  11.0 60.5 %copy-start.6 = (f32[8,256,256]{1,2,0:T(8,128)}, f32[8,256,256]{1,2,0:T(8,128)S(1)}, u32[]{:S(2)}) copy-start(f32[8,256,256]{1,2,0:T(8,128)S(1)} %get-tuple-element.17) | copy-start | bytes 6291460
  76.6 0.9 copy-start.1
  76.6 1.0 copy-start.2
  76.6 1.1 copy-start.3
  76.7 845.2 %all-reduce.2.cloned.1.call-start = ((), (), s32[]{:S(2)}) async-start(), calls=%async_computation.4 | async-start | bytes 131072 | tf_op jit(solution)/shard_map/psum | solution.py:100
  216.1 4.3 copy-start.7
Sparse Core Ops, SparseCore 0:
  10.1 61.2 all-gather.2
  74.5 141.5 all-gather.4
  220.5 638.9 reduce-scatter.1
  862.2 59.6 all-reduce.1
where the time goes:
time: 933 us; the launch traced here: 932 us
  waiting for transfers between devices  898 us (96%)
  between operations  13.9 us (1%)
  matrix products  12.5 us (1%)
    reduce_scatter x1, waiting for transfers between devices, per_device(): lax.psum_scatter(term.astype(jnp.bfloat16).astype(jnp.float32).astype(jnp...  637 us
    all_gather x1, waiting for transfers between devices, per_device(): lax.all_gather(value_weight, 'shard', axis=0, tiled=True)  138 us
    psum x1, waiting for transfers between devices, per_device(): summed = lax.psum(shard_part, 'replica').astype(jnp.float32)  61 us
    all_gather x1, waiting for transfers between devices, per_device(): gathered = lax.all_gather(activations, 'tensor', axis=1, tiled=True)  60.4 us
  transfers between devices with their start and end apart: 4, of which 4 were waited for; matrix products, arithmetic and copies ran while one was open for 2% of the time, Pallas kernels for 0%

commit v1 on v0

v1 whole, which is shorter than its diff:
```python
import functools
import math

import jax
import jax.numpy as jnp
from jax import lax
from jax.experimental import pallas as pl
from jax.experimental.pallas import tpu as pltpu
from jax.sharding import PartitionSpec as P

STEP = 10
BETA_FIRST = 0.9
BETA_SECOND = 0.95
LEARN_RATE = 0.001
WEIGHT_DECAY = 0.1
EPSILON = 1e-08

F32 = jnp.float32
BF16 = jnp.bfloat16
MESH = pl.DeviceIdType.MESH
TOK = 256
HD = 128
HEADS = 8
HALF = 1024
QTR = 256
RANKS = 128
FACTOR = 1.0 / math.sqrt(HD)
NT = (((1,), (1,)), ((), ()))


def place(x, y, z, c):
    return (y, (x // 2) * 16 + z, (x % 2) * 2 + c)


def kernel(
    act, que, key, gout, seg, wgt, mas, fst, snd,
    o_gq, o_gk, o_grad, o_mas, o_fst, o_snd,
    a2, qv, kv, gov, segv, masv, fstv, sndv,
    wbuf, bias, wst, gv, gt, tt, tmg, r1, sx, zr, rb, ob, gf,
    pp, pr, vs, vr, vals, ktr, gk, gqv, gkv, og, om, of, osn,
    ssem, rsem, lsem,
):
    y = lax.axis_index("tensor")
    s = lax.axis_index("shard")
    r = lax.axis_index("replica")
    z = s % 16
    c = r % 2
    x = (s // 16) * 2 + r // 2

    ids = [0]

    def new_id(n=1):
        ids[0] += n
        return ids[0] - n

    def send(src, dst, i, dev):
        cp = pltpu.make_async_remote_copy(
            src_ref=src, dst_ref=dst, send_sem=ssem.at[i], recv_sem=rsem.at[i],
            device_id=dev, device_id_type=MESH,
        )
        cp.start()
        sends.append((src, i))

    def got(ref, i):
        pltpu.make_async_copy(ref, ref, rsem.at[i]).wait()

    sends = []
    xr, xl = (x + 1) % 4, (x + 3) % 4
    xo = (x + 2) % 4
    c_dev = place(x, y, z, 1 - c)
    xr_dev, xl_dev = place(xr, y, z, c), place(xl, y, z, c)

    def y_dev(d):
        return place(x, (y + d) % 4, z, c)

    def z_dev(d):
        return place(x, y, (z + d + 16) % 16, c)

    s_y, s_c, s_x = s // 8, (s % 8) // 4, s % 4
    own_s, own_y = 8 * y + 4 * c + x, z % 4

    def rep_dev(k):
        return place(s_x, s_y, 4 * k + y, s_c)

    def owner_dev(k):
        return (own_y, own_s, k)

    is_self = jnp.logical_and(own_s == s, own_y == y)

    barrier = pltpu.get_barrier_semaphore()
    for dev in [c_dev, xr_dev, xl_dev, place(x + 1 - 2 * (x % 2), y, z, 1 - c)] + [
        y_dev(d) for d in (1, 2, 3)
    ] + [z_dev(d) for d in (-2, -1, 1, 2)]:
        pl.semaphore_signal(barrier, inc=1, device_id=dev, device_id_type=MESH)
    for k in range(4):
        @pl.when(jnp.logical_not(jnp.logical_and(is_self, k == r)))
        def _():
            pl.semaphore_signal(barrier, inc=1, device_id=owner_dev(k), device_id_type=MESH)

        @pl.when(jnp.logical_not(jnp.logical_and(is_self, k == z // 4)))
        def _():
            pl.semaphore_signal(barrier, inc=1, device_id=rep_dev(k), device_id_type=MESH)

    mine = pl.ds(pl.multiple_of(TOK * c, TOK), TOK)
    theirs = pl.ds(pl.multiple_of(TOK * (1 - c), TOK), TOK)
    loads = [
        (que, qv), (key, kv), (seg, segv), (gout, gov),
        (act.at[:, pl.ds(pl.multiple_of(HALF * c, HALF), HALF)], a2.at[mine]),
        (mas, masv), (fst, fstv), (snd, sndv),
    ]
    copies = [pltpu.make_async_copy(a, b, lsem.at[n]) for n, (a, b) in enumerate(loads)]
    for cp in copies:
        cp.start()

    pl.semaphore_wait(barrier, 19 - 2 * is_self.astype(jnp.int32))

    w1a = new_id()
    zy = pl.ds(pl.multiple_of(HD * y, HD), HD)
    send(wgt, wbuf.at[s_x, :, zy], w1a, rep_dev((r + 1) % 4))
    a_id = new_id()
    send(act.at[:, pl.ds(pl.multiple_of(HALF * (1 - c), HALF), HALF)], a2.at[mine], a_id, c_dev)

    for cp in copies[:4]:
        cp.wait()
    seg_row = jnp.broadcast_to(segv[...].astype(F32), (TOK, TOK))
    rows = lax.broadcasted_iota(jnp.int32, (TOK, TOK), 0)
    cols = lax.broadcasted_iota(jnp.int32, (TOK, TOK), 1)
    allowed = jnp.logical_and(seg_row.T == seg_row, rows <= cols)
    bias[...] = jnp.where(allowed, 0.0, -1e30)
    ktr[...] = kv[...].astype(F32).T.astype(BF16)

    def forward_head(h, acc):
        lanes = pl.ds(pl.multiple_of(h * HD, HD), HD)
        scores = lax.dot_general(kv[...], qv[:, lanes], NT, preferred_element_type=F32)
        scores = scores * FACTOR + bias[...]
        powered = jnp.exp(scores - jnp.max(scores, axis=0, keepdims=True))
        weights = powered * (1.0 / jnp.sum(powered, axis=0, keepdims=True))
        wst[h] = weights
        return acc + jnp.dot(weights.astype(BF16), gov[:, lanes], preferred_element_type=F32)

    acc = lax.fori_loop(0, HEADS // 2, forward_head, jnp.zeros((TOK, HD), F32))

    zo = pl.ds(pl.multiple_of(HD * own_y, HD), HD)
    got(wbuf.at[x, :, zo], w1a)
    w1b = new_id(3)
    for n, d in enumerate((-1, 1, 2)):
        send(wbuf.at[x, :, zo], wbuf.at[x, :, zo], w1b + n, z_dev(d))

    acc = lax.fori_loop(HEADS // 2, HEADS, forward_head, acc)
    gyt = pl.ds(pl.multiple_of(HD * y, HD), HD)
    gt[gyt, mine] = acc.T.astype(BF16)

    g_y = new_id(3)
    for d in (2, 1, 3):
        send(gt.at[gyt, mine], gt.at[gyt, mine], g_y + d - 1, y_dev(d))
    g_c = new_id(4)
    send(gt.at[gyt, mine], gt.at[gyt, mine], g_c, c_dev)

    for n, d in enumerate((-1, 1, 2)):
        zn = pl.ds(pl.multiple_of(HD * ((z - d + 16) % 4), HD), HD)
        got(wbuf.at[x, :, zn], w1b + n)
    lo, hi = pl.ds(0, HD), pl.ds(HD, HD)
    w2 = new_id(6)
    send(wbuf.at[x, lo], wbuf.at[x, lo], w2, xr_dev)
    send(wbuf.at[x, hi], wbuf.at[x, hi], w2 + 1, xl_dev)
    send(wbuf.at[x, hi], wbuf.at[x, hi], w2 + 2, xr_dev)
    send(wbuf.at[x, lo], wbuf.at[x, lo], w2 + 3, xl_dev)

    for d in (1, 3, 2):
        rows_d = pl.ds(pl.multiple_of(HD * ((y - d + 4) % 4), HD), HD)
        got(gt.at[rows_d, mine], g_y + d - 1)
        send(gt.at[rows_d, mine], gt.at[rows_d, mine], g_c + d, c_dev)
    for cp in copies[4:5]:
        cp.wait()
    got(a2.at[theirs], a_id)
    for n in range(4):
        rows_d = pl.ds(pl.multiple_of(HD * ((y - n + 4) % 4), HD), HD)
        got(gt.at[rows_d, theirs], g_c + n)

    def term(q, half):
        return jnp.dot(
            gt[pl.ds(2 * HD * half, 2 * HD), :],
            a2[:, pl.ds(pl.multiple_of(QTR * q, QTR), QTR)],
            preferred_element_type=F32,
        )

    top, bot = pl.ds(0, 2 * HD), pl.ds(2 * HD, 2 * HD)
    r1_id = new_id(6)
    tt[0] = term(xo, 0).astype(BF16)
    send(tt.at[0], r1.at[0], r1_id, xr_dev)
    tt[1] = term(xo, 1).astype(BF16)
    send(tt.at[1], r1.at[1], r1_id + 1, xl_dev)
    tt[2] = term(xr, 1).astype(BF16)
    send(tt.at[2], r1.at[2], r1_id + 2, xr_dev)
    tt[3] = term(xl, 0).astype(BF16)
    send(tt.at[3], r1.at[3], r1_id + 3, xl_dev)

    got(wbuf.at[xl, lo], w2)
    send(wbuf.at[xl, lo], wbuf.at[xl, lo], w2 + 4, xr_dev)
    got(wbuf.at[xr, hi], w2 + 1)
    send(wbuf.at[xr, hi], wbuf.at[xr, hi], w2 + 5, xl_dev)

    tmg[0] = term(xr, 0)
    tmg[1] = term(xl, 1)
    got(r1.at[0], r1_id)
    tt[4] = (tmg[0] + r1[0].astype(F32)).astype(BF16)
    send(tt.at[4], r1.at[4], r1_id + 4, xr_dev)
    got(r1.at[1], r1_id + 1)
    tt[5] = (tmg[1] + r1[1].astype(F32)).astype(BF16)
    send(tt.at[5], r1.at[5], r1_id + 5, xl_dev)
    sx[top, :] = term(x, 0)
    sx[bot, :] = term(x, 1)

    def values_of(q, first):
        part = jnp.dot(
            a2[:, pl.ds(pl.multiple_of(QTR * q, QTR), QTR)], wbuf[q], preferred_element_type=F32
        )
        pp[...] = part if first else pp[...] + part

    values_of(x, True)
    got(wbuf.at[xl, hi], w2 + 2)
    values_of(xl, False)
    got(wbuf.at[xr, lo], w2 + 3)
    values_of(xr, False)

    got(r1.at[3], r1_id + 3)
    got(r1.at[2], r1_id + 2)
    got(r1.at[4], r1_id + 4)
    got(r1.at[5], r1_id + 5)
    sx[top, :] = sx[top, :] + (r1[3].astype(F32) + r1[4].astype(F32))
    sx[bot, :] = sx[bot, :] + (r1[2].astype(F32) + r1[5].astype(F32))
    z_id = new_id(3)
    for n, d in enumerate((-2, -1, 1)):
        part = pl.ds(pl.multiple_of(HD * ((z + d + 16) % 4), HD), HD)
        zr[3 + n] = sx[part, :].astype(BF16)
        send(zr.at[3 + n], zr.at[n], z_id + n, z_dev(d))

    got(wbuf.at[xo, lo], w2 + 4)
    got(wbuf.at[xo, hi], w2 + 5)
    values_of(xo, False)
    v1 = new_id()
    send(pp.at[theirs], pr, v1, c_dev)

    for n in range(3):
        got(zr.at[n], z_id + n)
    part = pl.ds(pl.multiple_of(HD * own_y, HD), HD)
    rb[...] = (
        sx[part, :] + zr[0].astype(F32) + zr[1].astype(F32) + zr[2].astype(F32)
    ).astype(BF16)
    o_id = new_id(4)
    for k in range(4):
        src = rb.at[pl.ds(32 * k, 32)]
        stay = jnp.logical_and(is_self, k == r)

        @pl.when(jnp.logical_not(stay))
        def _():
            pltpu.make_async_remote_copy(
                src_ref=src, dst_ref=ob.at[z // 4], send_sem=ssem.at[o_id + k],
                recv_sem=rsem.at[o_id + z // 4], device_id=owner_dev(k), device_id_type=MESH,
            ).start()

        @pl.when(stay)
        def _():
            pltpu.make_async_copy(src, ob.at[z // 4], rsem.at[o_id + z // 4]).start()

    got(pr, v1)
    both = pp[mine, :] + pr[...]
    vs[...] = both.astype(BF16)
    pp[mine, :] = both
    v2 = new_id(3)
    for d in (2, 1, 3):
        lanes = pl.ds(pl.multiple_of(HD * ((y + d) % 4), HD), HD)
        send(vs.at[:, lanes], vr.at[d - 1], v2 + d - 1, y_dev(d))

    for k in range(4):
        got(ob.at[k], o_id + k)
    quarter = pl.ds(pl.multiple_of(32 * r, 32), 32)
    gf[quarter, :] = (
        ob[0].astype(F32) + ob[1].astype(F32) + ob[2].astype(F32) + ob[3].astype(F32)
    ) * (1.0 / RANKS)
    f_id = new_id(3)
    for d in (1, 2, 3):
        rd = (r + d) % 4
        send(gf.at[quarter], gf.at[quarter], f_id + d - 1, (y, s, rd))

    for d in (1, 2, 3):
        got(vr.at[d - 1], v2 + d - 1)
    vals[...] = (
        pp[mine, zy] + vr[0].astype(F32) + vr[1].astype(F32) + vr[2].astype(F32)
    ).astype(BF16)

    def backward_head(h, acc):
        lanes = pl.ds(pl.multiple_of(h * HD, HD), HD)
        gw = lax.dot_general(vals[...], gov[:, lanes], NT, preferred_element_type=F32)
        weights = wst[h]
        dots = jnp.sum(weights.astype(BF16).astype(F32) * gw, axis=0, keepdims=True)
        gs = (weights * (gw - dots) * FACTOR).astype(BF16)
        gq = jnp.dot(ktr[...], gs, preferred_element_type=F32)
        gqv[:, lanes] = gq.T.astype(BF16)
        return acc + jnp.dot(gs, qv[:, lanes], preferred_element_type=F32)

    gkv[...] = lax.fori_loop(0, HEADS, backward_head, jnp.zeros((TOK, HD), F32)).astype(BF16)
    outs = [pltpu.make_async_copy(gqv, o_gq, lsem.at[8]), pltpu.make_async_copy(gkv, o_gk, lsem.at[9])]
    for cp in outs:
        cp.start()

    for d in (1, 2, 3):
        other = pl.ds(pl.multiple_of(32 * ((r - d + 4) % 4), 32), 32)
        got(gf.at[other], f_id + d - 1)
    for cp in copies[5:]:
        cp.wait()
    gradient = gf[...].T
    new_first = BETA_FIRST * fstv[...] + (1.0 - BETA_FIRST) * gradient
    new_second = BETA_SECOND * sndv[...] + (1.0 - BETA_SECOND) * gradient * gradient
    corrected = (
        new_first
        / (1.0 - BETA_FIRST**STEP)
        / (jnp.sqrt(new_second / (1.0 - BETA_SECOND**STEP)) + EPSILON)
    )
    og[...] = gradient
    om[...] = masv[...] - LEARN_RATE * (corrected + WEIGHT_DECAY * masv[...])
    of[...] = new_first
    osn[...] = new_second
    for n, (a, b) in enumerate(((og, o_grad), (om, o_mas), (of, o_fst), (osn, o_snd))):
        cp = pltpu.make_async_copy(a, b, lsem.at[10 + n])
        cp.start()
        outs.append(cp)

    for src, i in sends:
        pltpu.make_async_copy(src, src, ssem.at[i]).wait()
    for k in range(4):
        src = rb.at[pl.ds(32 * k, 32)]

        @pl.when(jnp.logical_not(jnp.logical_and(is_self, k == r)))
        def _():
            pltpu.make_async_copy(src, src, ssem.at[o_id + k]).wait()
    for cp in outs:
        cp.wait()


N_SEM = 48


def per_device(act, que, key, gout, seg, wgt, mas, fst, snd):
    sds = jax.ShapeDtypeStruct
    any_spec = pl.BlockSpec(memory_space=pl.ANY)
    vm = pltpu.VMEM
    shard = (QTR, HD)
    return pl.pallas_call(
        kernel,
        out_shape=(
            sds((TOK, HALF), BF16), sds((TOK, HD), BF16),
            sds(shard, F32), sds(shard, F32), sds(shard, F32), sds(shard, F32),
        ),
        in_specs=[any_spec] * 9,
        out_specs=[any_spec] * 6,
        scratch_shapes=[
            vm((2 * TOK, HALF), BF16),
            vm((TOK, HEADS * HD), BF16), vm((TOK, HD), BF16), vm((TOK, HEADS * HD), BF16),
            vm((1, TOK), jnp.int32), vm(shard, F32), vm(shard, F32), vm(shard, F32),
            vm((4, QTR, 4 * HD), BF16),
            vm((TOK, TOK), F32),
            vm((HEADS, TOK, TOK), F32),
            vm((TOK, HD), F32),
            vm((4 * HD, 2 * TOK), BF16),
            vm((6, 2 * HD, QTR), BF16),
            vm((2, 2 * HD, QTR), F32),
            vm((6, 2 * HD, QTR), BF16),
            vm((4 * HD, QTR), F32),
            vm((6, HD, QTR), BF16),
            vm((HD, QTR), BF16),
            vm((4, 32, QTR), BF16),
            vm((HD, QTR), F32),
            vm((2 * TOK, 4 * HD), F32),
            vm((TOK, 4 * HD), F32),
            vm((TOK, 4 * HD), BF16),
            vm((3, TOK, HD), BF16),
            vm((TOK, HD), BF16),
            vm((HD, TOK), BF16),
            vm((TOK, HD), F32),
            vm((TOK, HEADS * HD), BF16), vm((TOK, HD), BF16),
            vm(shard, F32), vm(shard, F32), vm(shard, F32), vm(shard, F32),
            pltpu.SemaphoreType.DMA((N_SEM,)),
            pltpu.SemaphoreType.DMA((N_SEM,)),
            pltpu.SemaphoreType.DMA((16,)),
        ],
        compiler_params=pltpu.CompilerParams(
            collective_id=0, has_side_effects=True, vmem_limit_bytes=40 << 20
        ),
    )(act, que, key, gout, seg.reshape(1, TOK), wgt, mas, fst, snd)


def solution(mesh):
    token = P(("shard", "replica"), "tensor")
    row = P("shard", "tensor")
    return jax.shard_map(
        per_device,
        mesh=mesh,
        in_specs=(token, token, token, token, P(("shard", "replica")), row, row, row, row),
        out_specs=(token, token, row, row, row, row),
        check_vma=False,
    )
```

time: 933 us -> 89.3 us (0.10)
  the two profiles are of different devices: /device:TPU:1 before, /device:TPU:121 now
where the time goes in v1:
time: 89.3 us; the launch traced here: 88.9 us
  Pallas kernels  75.8 us (85%)
  local copies, waits for them, and re-layouts  12.4 us (14%)
    pallas_call x1, Pallas kernels, per_device(): pl.pallas_call(kernel, out_shape=(sds((TOK, HALF), BF16), sds((TOK, HD),...  75.8 us
    unnamed x24, local copies, waits for them, and re-layouts  12.4 us

profile of v1, /device:TPU:121, one launch (start us, length us, event | category | flops | bytes accessed | tf_op | source)
XLA Modules:
  0.0 88.9 jit_solution(17322076112747256991)
XLA Ops:
  0.6 0.0 copy-start.8
  0.6 0.7 copy-done.8
  1.3 0.0 copy-start
  1.3 1.2 %copy-done = bf16[256,2048]{1,0:T(8,128)(2,1)S(1)} copy-done((bf16[256,2048]{1,0:T(8,128)(2,1)S(1)}, bf16[256,2048]{1,0:T(8,128)(2,1)}, u32[]{:S(2)}) %copy-start) | copy-done | bytes 1048600
  2.5 0.0 copy-start.1
  2.5 1.0 %copy-done.1 = bf16[256,1024]{1,0:T(8,128)(2,1)S(1)} copy-done((bf16[256,1024]{1,0:T(8,128)(2,1)S(1)}, bf16[256,1024]{1,0:T(8,128)(2,1)}, u32[]{:S(2)}) %copy-start.1) | copy-done | bytes 524312
  3.6 0.0 copy-start.2
  3.6 1.0 %copy-done.2 = bf16[256,1024]{1,0:T(8,128)(2,1)S(1)} copy-done((bf16[256,1024]{1,0:T(8,128)(2,1)S(1)}, bf16[256,1024]{1,0:T(8,128)(2,1)}, u32[]{:S(2)}) %copy-start.2) | copy-done | bytes 524312
  4.6 0.0 copy-start.3
  4.6 0.9 %copy-done.3 = f32[256,128]{1,0:T(8,128)S(1)} copy-done((f32[256,128]{1,0:T(8,128)S(1)}, f32[256,128]{1,0:T(8,128)}, u32[]{:S(2)}) %copy-start.3) | copy-done | bytes 131096
  5.5 0.0 copy-start.4
  5.5 0.9 %copy-done.4 = f32[256,128]{1,0:T(8,128)S(1)} copy-done((f32[256,128]{1,0:T(8,128)S(1)}, f32[256,128]{1,0:T(8,128)}, u32[]{:S(2)}) %copy-start.4) | copy-done | bytes 131096
  6.4 0.0 copy-start.5
  6.4 0.9 %copy-done.5 = f32[256,128]{1,0:T(8,128)S(1)} copy-done((f32[256,128]{1,0:T(8,128)S(1)}, f32[256,128]{1,0:T(8,128)}, u32[]{:S(2)}) %copy-start.5) | copy-done | bytes 131096
  7.3 0.0 copy-start.6
  7.3 0.8 copy-done.6
  8.2 0.0 copy-start.7
  8.2 0.8 copy-done.7
  9.0 75.8 %shard_map.136 = (bf16[256,1024]{1,0:T(8,128)(2,1)S(1)}, bf16[256,128]{1,0:T(8,128)(2,1)S(1)}, f32[256,128]{1,0:T(8,128)S(1)}, f32[256,128]{1,0:T(8,128)S(1)}, f...) custom-call(bf16[256,2048]{1,0:T(8,128)(2,1)S(1)} %copy-done, bf16[256,1024]{1,0:T(8,128)(2,1)S(1)} %copy-done.1, ...), custom_call_target="tpu_custom_call" | custom-call | tf_op jit(solution)/shard_map/pallas_call | solution.py:349
  84.8 0.8 copy.21
  85.6 0.6 copy.22
  86.2 0.7 copy.23
  86.9 0.7 copy.24
  87.5 0.7 copy.25
  88.2 0.7 copy.26
Async XLA Ops:
  0.6 0.7 copy-start.8
  1.3 1.2 %copy-start = (bf16[256,2048]{1,0:T(8,128)(2,1)S(1)}, bf16[256,2048]{1,0:T(8,128)(2,1)}, u32[]{:S(2)}) copy-start(bf16[256,2048]{1,0:T(8,128)(2,1)} %act.1) | copy-start | bytes 3145732
  2.5 1.0 %copy-start.1 = (bf16[256,1024]{1,0:T(8,128)(2,1)S(1)}, bf16[256,1024]{1,0:T(8,128)(2,1)}, u32[]{:S(2)}) copy-start(bf16[256,1024]{1,0:T(8,128)(2,1)} %que.1) | copy-start | bytes 1572868
  3.6 1.0 %copy-start.2 = (bf16[256,1024]{1,0:T(8,128)(2,1)S(1)}, bf16[256,1024]{1,0:T(8,128)(2,1)}, u32[]{:S(2)}) copy-start(bf16[256,1024]{1,0:T(8,128)(2,1)} %gout.1) | copy-start | bytes 1572868
  4.6 0.9 %copy-start.3 = (f32[256,128]{1,0:T(8,128)S(1)}, f32[256,128]{1,0:T(8,128)}, u32[]{:S(2)}) copy-start(f32[256,128]{1,0:T(8,128)} %mas.1) | copy-start | bytes 393220
  5.5 0.9 %copy-start.4 = (f32[256,128]{1,0:T(8,128)S(1)}, f32[256,128]{1,0:T(8,128)}, u32[]{:S(2)}) copy-start(f32[256,128]{1,0:T(8,128)} %fst.1) | copy-start | bytes 393220
  6.4 0.9 %copy-start.5 = (f32[256,128]{1,0:T(8,128)S(1)}, f32[256,128]{1,0:T(8,128)}, u32[]{:S(2)}) copy-start(f32[256,128]{1,0:T(8,128)} %snd.1) | copy-start | bytes 393220
  7.3 0.8 copy-start.6
  8.2 0.8 copy-start.7

commit v2 on v1

--- a/solution.py
+++ b/solution.py
@@ -76,11 +76,12 @@
     def z_dev(d):
         return place(x, y, (z + d + 16) % 16, c)
 
-    s_y, s_c, s_x = s // 8, (s % 8) // 4, s % 4
-    own_s, own_y = 8 * y + 4 * c + x, z % 4
+    s_y, s_c, s_q = s // 8, (s % 8) // 4, s % 4
+    own_q = z % 4
+    own_s, own_y = 8 * y + 4 * c + own_q, x
 
     def rep_dev(k):
-        return place(s_x, s_y, 4 * k + y, s_c)
+        return place(y, s_y, 4 * k + s_q, s_c)
 
     def owner_dev(k):
         return (own_y, own_s, k)
@@ -112,14 +113,6 @@
     for cp in copies:
         cp.start()
 
-    pl.semaphore_wait(barrier, 19 - 2 * is_self.astype(jnp.int32))
-
-    w1a = new_id()
-    zy = pl.ds(pl.multiple_of(HD * y, HD), HD)
-    send(wgt, wbuf.at[s_x, :, zy], w1a, rep_dev((r + 1) % 4))
-    a_id = new_id()
-    send(act.at[:, pl.ds(pl.multiple_of(HALF * (1 - c), HALF), HALF)], a2.at[mine], a_id, c_dev)
-
     for cp in copies[:4]:
         cp.wait()
     seg_row = jnp.broadcast_to(segv[...].astype(F32), (TOK, TOK))
@@ -138,17 +131,11 @@
         wst[h] = weights
         return acc + jnp.dot(weights.astype(BF16), gov[:, lanes], preferred_element_type=F32)
 
-    acc = lax.fori_loop(0, HEADS // 2, forward_head, jnp.zeros((TOK, HD), F32))
-
-    zo = pl.ds(pl.multiple_of(HD * own_y, HD), HD)
-    got(wbuf.at[x, :, zo], w1a)
-    w1b = new_id(3)
-    for n, d in enumerate((-1, 1, 2)):
-        send(wbuf.at[x, :, zo], wbuf.at[x, :, zo], w1b + n, z_dev(d))
-
-    acc = lax.fori_loop(HEADS // 2, HEADS, forward_head, acc)
+    acc = lax.fori_loop(0, HEADS, forward_head, jnp.zeros((TOK, HD), F32))
     gyt = pl.ds(pl.multiple_of(HD * y, HD), HD)
     gt[gyt, mine] = acc.T.astype(BF16)
+
+    pl.semaphore_wait(barrier, 19 - 2 * is_self.astype(jnp.int32))
 
     g_y = new_id(3)
     for d in (2, 1, 3):
@@ -156,22 +143,20 @@
     g_c = new_id(4)
     send(gt.at[gyt, mine], gt.at[gyt, mine], g_c, c_dev)
 
-    for n, d in enumerate((-1, 1, 2)):
-        zn = pl.ds(pl.multiple_of(HD * ((z - d + 16) % 4), HD), HD)
-        got(wbuf.at[x, :, zn], w1b + n)
-    lo, hi = pl.ds(0, HD), pl.ds(HD, HD)
-    w2 = new_id(6)
-    send(wbuf.at[x, lo], wbuf.at[x, lo], w2, xr_dev)
-    send(wbuf.at[x, hi], wbuf.at[x, hi], w2 + 1, xl_dev)
-    send(wbuf.at[x, hi], wbuf.at[x, hi], w2 + 2, xr_dev)
-    send(wbuf.at[x, lo], wbuf.at[x, lo], w2 + 3, xl_dev)
+    w1a = new_id()
+    step = (r - 2 * (y % 2) - s_c + 9) % 4
+    send(
+        wgt, wbuf.at[y, pl.ds(pl.multiple_of(QTR * s_q, QTR), QTR)], w1a,
+        place(y, s_y, (z + 4 * step) % 16, s_c),
+    )
+    a_id = new_id()
+    send(act.at[:, pl.ds(pl.multiple_of(HALF * (1 - c), HALF), HALF)], a2.at[mine], a_id, c_dev)
 
     for d in (1, 3, 2):
         rows_d = pl.ds(pl.multiple_of(HD * ((y - d + 4) % 4), HD), HD)
         got(gt.at[rows_d, mine], g_y + d - 1)
         send(gt.at[rows_d, mine], gt.at[rows_d, mine], g_c + d, c_dev)
-    for cp in copies[4:5]:
-        cp.wait()
+    copies[4].wait()
     got(a2.at[theirs], a_id)
     for n in range(4):
         rows_d = pl.ds(pl.multiple_of(HD * ((y - n + 4) % 4), HD), HD)
@@ -179,12 +164,11 @@
 
     def term(q, half):
         return jnp.dot(
-            gt[pl.ds(2 * HD * half, 2 * HD), :],
-            a2[:, pl.ds(pl.multiple_of(QTR * q, QTR), QTR)],
+            gt[pl.ds(pl.multiple_of(HD * q, HD), HD), :],
+            a2[:, HALF // 2 * half : HALF // 2 * (half + 1)],
             preferred_element_type=F32,
         )
 
-    top, bot = pl.ds(0, 2 * HD), pl.ds(2 * HD, 2 * HD)
     r1_id = new_id(6)
     tt[0] = term(xo, 0).astype(BF16)
     send(tt.at[0], r1.at[0], r1_id, xr_dev)
@@ -194,58 +178,68 @@
     send(tt.at[2], r1.at[2], r1_id + 2, xr_dev)
     tt[3] = term(xl, 0).astype(BF16)
     send(tt.at[3], r1.at[3], r1_id + 3, xl_dev)
-
-    got(wbuf.at[xl, lo], w2)
-    send(wbuf.at[xl, lo], wbuf.at[xl, lo], w2 + 4, xr_dev)
-    got(wbuf.at[xr, hi], w2 + 1)
-    send(wbuf.at[xr, hi], wbuf.at[xr, hi], w2 + 5, xl_dev)
-
     tmg[0] = term(xr, 0)
     tmg[1] = term(xl, 1)
+
+    def quarter_of(q):
+        return pl.ds(pl.multiple_of(QTR * (q % 4), QTR), QTR)
+
+    side = 1 - 2 * (z % 2)
+    mine_q = wbuf.at[x, quarter_of(own_q)]
+    got(mine_q, w1a)
+    w1b = new_id(3)
+    send(mine_q, mine_q, w1b, z_dev(2 * side))
+    send(mine_q, mine_q, w1b + 1, z_dev(1))
+    send(mine_q, mine_q, w1b + 2, z_dev(-1))
+
+    top, bot = slice(0, HALF // 2), slice(HALF // 2, HALF)
+    sx[:, top] = term(x, 0)
+    sx[:, bot] = term(x, 1)
     got(r1.at[0], r1_id)
     tt[4] = (tmg[0] + r1[0].astype(F32)).astype(BF16)
     send(tt.at[4], r1.at[4], r1_id + 4, xr_dev)
     got(r1.at[1], r1_id + 1)
     tt[5] = (tmg[1] + r1[1].astype(F32)).astype(BF16)
     send(tt.at[5], r1.at[5], r1_id + 5, xl_dev)
-    sx[top, :] = term(x, 0)
-    sx[bot, :] = term(x, 1)
-
-    def values_of(q, first):
-        part = jnp.dot(
-            a2[:, pl.ds(pl.multiple_of(QTR * q, QTR), QTR)], wbuf[q], preferred_element_type=F32
-        )
-        pp[...] = part if first else pp[...] + part
-
-    values_of(x, True)
-    got(wbuf.at[xl, hi], w2 + 2)
-    values_of(xl, False)
-    got(wbuf.at[xr, lo], w2 + 3)
-    values_of(xr, False)
+
+    got(wbuf.at[x, quarter_of(z - 1 + 4)], w1b + 1)
+    got(wbuf.at[x, quarter_of(z + 1)], w1b + 2)
+    got(wbuf.at[x, quarter_of(z + 2)], w1b)
+    lo, hi = pl.ds(0, HALF // 2), pl.ds(HALF // 2, HALF // 2)
+    w2 = new_id(6)
+    send(wbuf.at[x, lo], wbuf.at[x, lo], w2, xr_dev)
+    send(wbuf.at[x, hi], wbuf.at[x, hi], w2 + 1, xl_dev)
+    send(wbuf.at[x, hi], wbuf.at[x, hi], w2 + 2, xr_dev)
+    send(wbuf.at[x, lo], wbuf.at[x, lo], w2 + 3, xl_dev)
+
+    v1 = new_id(4)
+
+    def values_of(q, n):
+        pp[q] = jnp.dot(a2[...], wbuf[q], preferred_element_type=F32)
+        send(pp.at[q, theirs], pr.at[q], v1 + n, c_dev)
 
     got(r1.at[3], r1_id + 3)
     got(r1.at[2], r1_id + 2)
     got(r1.at[4], r1_id + 4)
     got(r1.at[5], r1_id + 5)
-    sx[top, :] = sx[top, :] + (r1[3].astype(F32) + r1[4].astype(F32))
-    sx[bot, :] = sx[bot, :] + (r1[2].astype(F32) + r1[5].astype(F32))
+    sx[:, top] = sx[:, top] + (r1[3].astype(F32) + r1[4].astype(F32))
+    sx[:, bot] = sx[:, bot] + (r1[2].astype(F32) + r1[5].astype(F32))
     z_id = new_id(3)
-    for n, d in enumerate((-2, -1, 1)):
-        part = pl.ds(pl.multiple_of(HD * ((z + d + 16) % 4), HD), HD)
-        zr[3 + n] = sx[part, :].astype(BF16)
+    for n, d in enumerate((-2 * side, 1, -1)):
+        zr[3 + n] = sx[:, quarter_of(z + d + 16)].astype(BF16)
         send(zr.at[3 + n], zr.at[n], z_id + n, z_dev(d))
 
-    got(wbuf.at[xo, lo], w2 + 4)
-    got(wbuf.at[xo, hi], w2 + 5)
-    values_of(xo, False)
-    v1 = new_id()
-    send(pp.at[theirs], pr, v1, c_dev)
+    values_of(x, 0)
+    got(wbuf.at[xl, lo], w2)
+    send(wbuf.at[xl, lo], wbuf.at[xl, lo], w2 + 4, xr_dev)
+    got(wbuf.at[xr, hi], w2 + 1)
+    send(wbuf.at[xr, hi], wbuf.at[xr, hi], w2 + 5, xl_dev)
 
     for n in range(3):
         got(zr.at[n], z_id + n)
-    part = pl.ds(pl.multiple_of(HD * own_y, HD), HD)
     rb[...] = (
-        sx[part, :] + zr[0].astype(F32) + zr[1].astype(F32) + zr[2].astype(F32)
+        sx[:, quarter_of(own_q)]
+        + zr[0].astype(F32) + zr[1].astype(F32) + zr[2].astype(F32)
     ).astype(BF16)
     o_id = new_id(4)
     for k in range(4):
@@ -263,14 +257,21 @@
         def _():
             pltpu.make_async_copy(src, ob.at[z // 4], rsem.at[o_id + z // 4]).start()
 
-    got(pr, v1)
-    both = pp[mine, :] + pr[...]
-    vs[...] = both.astype(BF16)
-    pp[mine, :] = both
+    got(wbuf.at[xl, hi], w2 + 2)
+    values_of(xl, 1)
+    got(wbuf.at[xr, lo], w2 + 3)
+    values_of(xr, 2)
+    got(wbuf.at[xo, lo], w2 + 4)
+    got(wbuf.at[xo, hi], w2 + 5)
+    values_of(xo, 3)
+
+    for n, q in ((0, x), (2, xl), (1, xr), (3, xo)):
+        got(pr.at[q], v1 + n)
     v2 = new_id(3)
     for d in (2, 1, 3):
-        lanes = pl.ds(pl.multiple_of(HD * ((y + d) % 4), HD), HD)
-        send(vs.at[:, lanes], vr.at[d - 1], v2 + d - 1, y_dev(d))
+        q = (y + d) % 4
+        vs[d - 1] = (pp[q, mine] + pr[q]).astype(BF16)
+        send(vs.at[d - 1], vr.at[d - 1], v2 + d - 1, y_dev(d))
 
     for k in range(4):
         got(ob.at[k], o_id + k)
@@ -286,7 +287,7 @@
     for d in (1, 2, 3):
         got(vr.at[d - 1], v2 + d - 1)
     vals[...] = (
-        pp[mine, zy] + vr[0].astype(F32) + vr[1].astype(F32) + vr[2].astype(F32)
+        pp[y, mine] + pr[y] + vr[0].astype(F32) + vr[1].astype(F32) + vr[2].astype(F32)
     ).astype(BF16)
 
     def backward_head(h, acc):
@@ -358,22 +359,22 @@
             vm((2 * TOK, HALF), BF16),
             vm((TOK, HEADS * HD), BF16), vm((TOK, HD), BF16), vm((TOK, HEADS * HD), BF16),
             vm((1, TOK), jnp.int32), vm(shard, F32), vm(shard, F32), vm(shard, F32),
-            vm((4, QTR, 4 * HD), BF16),
+            vm((4, HALF, HD), BF16),
             vm((TOK, TOK), F32),
             vm((HEADS, TOK, TOK), F32),
             vm((TOK, HD), F32),
             vm((4 * HD, 2 * TOK), BF16),
-            vm((6, 2 * HD, QTR), BF16),
-            vm((2, 2 * HD, QTR), F32),
-            vm((6, 2 * HD, QTR), BF16),
-            vm((4 * HD, QTR), F32),
+            vm((6, HD, HALF // 2), BF16),
+            vm((2, HD, HALF // 2), F32),
+            vm((6, HD, HALF // 2), BF16),
+            vm((HD, HALF), F32),
             vm((6, HD, QTR), BF16),
             vm((HD, QTR), BF16),
             vm((4, 32, QTR), BF16),
             vm((HD, QTR), F32),
-            vm((2 * TOK, 4 * HD), F32),
-            vm((TOK, 4 * HD), F32),
-            vm((TOK, 4 * HD), BF16),
+            vm((4, 2 * TOK, HD), F32),
+            vm((4, TOK, HD), F32),
+            vm((3, TOK, HD), BF16),
             vm((3, TOK, HD), BF16),
             vm((TOK, HD), BF16),
             vm((HD, TOK), BF16),
@@ -385,7 +386,7 @@
             pltpu.SemaphoreType.DMA((16,)),
         ],
         compiler_params=pltpu.CompilerParams(
-            collective_id=0, has_side_effects=True, vmem_limit_bytes=40 << 20
+            collective_id=0, has_side_effects=True, vmem_limit_bytes=60 << 20
         ),
     )(act, que, key, gout, seg.reshape(1, TOK), wgt, mas, fst, snd)
 

time: 89.3 us -> 65.8 us (0.74)
  the two profiles are of different devices: /device:TPU:121 before, /device:TPU:1 now
where the time goes in v2:
time: 65.8 us; the launch traced here: 65 us
  Pallas kernels  58 us (88%)
  local copies, waits for them, and re-layouts  6.34 us (10%)
  between operations  0.66 us (1%)
    pallas_call x1, Pallas kernels, per_device(): pl.pallas_call(kernel, out_shape=(sds((TOK, HALF), BF16), sds((TOK, HD),...  58 us
    unnamed x16, local copies, waits for them, and re-layouts  6.34 us

profile of v2, /device:TPU:1, one launch (start us, length us, event | category | flops | bytes accessed | tf_op | source)
XLA Modules:
  0.0 65.0 jit_solution(13068204517947225806)
XLA Ops:
  0.6 58.0 %shard_map.136 = (bf16[256,1024]{1,0:T(8,128)(2,1)}, bf16[256,128]{1,0:T(8,128)(2,1)}, f32[256,128]{1,0:T(8,128)}, f32[256,128]{1,0:T(8,128)}, f32[256,128]{1,0:T(8,128)}, /*index=5*/f32[256,128]{1,0:T(8,128)}) custom-call(bf16[256,2048]{1,0:T(8,128)(2,1)} %act.1, bf16[256,1024]{1,0:T(8,128)(2,1)} %que.1, bf16[256,128]{1,0:T(8,128)(2,1)} %key.1, ...), custom_call_target="tpu_custom_call" | custom-call | tf_op jit(solution)/shard_map/pallas_call | solution.py:350
  58.7 0.0 copy-start.4
  58.7 1.9 %copy.21 = bf16[256,1024]{1,0:T(8,128)(2,1)} copy(bf16[256,1024]{1,0:T(8,128)(2,1)} %get-tuple-element.12) | data formatting | bytes 1048576
  60.6 0.0 copy-done.4
  60.6 0.0 copy-start.3
  60.6 0.6 copy.22
  61.2 0.3 copy-done.3
  61.5 0.0 copy-start.2
  61.5 0.7 %copy.23 = f32[256,128]{1,0:T(8,128)} copy(f32[256,128]{1,0:T(8,128)S(1)} %copy-done.3) | data formatting | bytes 262144
  62.2 0.3 copy-done.2
  62.5 0.0 copy-start.1
  62.5 0.7 %copy.24 = f32[256,128]{1,0:T(8,128)} copy(f32[256,128]{1,0:T(8,128)S(1)} %copy-done.2) | data formatting | bytes 262144
  63.1 0.3 copy-done.1
  63.4 0.0 copy-start
  63.4 0.7 %copy.25 = f32[256,128]{1,0:T(8,128)} copy(f32[256,128]{1,0:T(8,128)S(1)} %copy-done.1) | data formatting | bytes 262144
  64.1 0.3 copy-done
  64.4 0.7 %copy.26 = f32[256,128]{1,0:T(8,128)} copy(f32[256,128]{1,0:T(8,128)S(1)} %copy-done) | data formatting | bytes 262144
Async XLA Ops:
  58.7 1.9 %copy-start.4 = (bf16[256,128]{1,0:T(8,128)(2,1)S(1)}, bf16[256,128]{1,0:T(8,128)(2,1)}, u32[]{:S(2)}) copy-start(bf16[256,128]{1,0:T(8,128)(2,1)} %get-tuple-element.13) | copy-start | bytes 196612
  60.6 0.9 %copy-start.3 = (f32[256,128]{1,0:T(8,128)S(1)}, f32[256,128]{1,0:T(8,128)}, u32[]{:S(2)}) copy-start(f32[256,128]{1,0:T(8,128)} %get-tuple-element.14) | copy-start | bytes 393220
  61.5 1.0 %copy-start.2 = (f32[256,128]{1,0:T(8,128)S(1)}, f32[256,128]{1,0:T(8,128)}, u32[]{:S(2)}) copy-start(f32[256,128]{1,0:T(8,128)} %get-tuple-element.15) | copy-start | bytes 393220
  62.5 1.0 %copy-start.1 = (f32[256,128]{1,0:T(8,128)S(1)}, f32[256,128]{1,0:T(8,128)}, u32[]{:S(2)}) copy-start(f32[256,128]{1,0:T(8,128)} %get-tuple-element.16) | copy-start | bytes 393220
  63.4 1.0 %copy-start = (f32[256,128]{1,0:T(8,128)S(1)}, f32[256,128]{1,0:T(8,128)}, u32[]{:S(2)}) copy-start(f32[256,128]{1,0:T(8,128)} %get-tuple-element.17) | copy-start | bytes 393220

commit v3 on v2

--- a/solution.py
+++ b/solution.py
@@ -24,6 +24,7 @@
 HALF = 1024
 QTR = 256
 RANKS = 128
+CH = 64
 FACTOR = 1.0 / math.sqrt(HD)
 NT = (((1,), (1,)), ((), ()))
 
@@ -131,26 +132,27 @@
         wst[h] = weights
         return acc + jnp.dot(weights.astype(BF16), gov[:, lanes], preferred_element_type=F32)
 
-    acc = lax.fori_loop(0, HEADS, forward_head, jnp.zeros((TOK, HD), F32))
+    acc = lax.fori_loop(0, 6, forward_head, jnp.zeros((TOK, HD), F32), unroll=2)
+    pl.semaphore_wait(barrier, 19 - 2 * is_self.astype(jnp.int32))
+
+    w1a = new_id(2)
+    step = (r - 2 * (y % 2) - s_c + 9) % 4
+    for p in range(2):
+        send(
+            wgt.at[pl.ds(HD * p, HD)], wbuf.at[y, s_q, p], w1a + p,
+            place(y, s_y, (z + 4 * step) % 16, s_c),
+        )
+    a_id = new_id()
+    send(act.at[:, pl.ds(pl.multiple_of(HALF * (1 - c), HALF), HALF)], a2.at[mine], a_id, c_dev)
+
+    acc = lax.fori_loop(6, HEADS, forward_head, acc, unroll=2)
     gyt = pl.ds(pl.multiple_of(HD * y, HD), HD)
     gt[gyt, mine] = acc.T.astype(BF16)
-
-    pl.semaphore_wait(barrier, 19 - 2 * is_self.astype(jnp.int32))
-
     g_y = new_id(3)
     for d in (2, 1, 3):
         send(gt.at[gyt, mine], gt.at[gyt, mine], g_y + d - 1, y_dev(d))
     g_c = new_id(4)
     send(gt.at[gyt, mine], gt.at[gyt, mine], g_c, c_dev)
-
-    w1a = new_id()
-    step = (r - 2 * (y % 2) - s_c + 9) % 4
-    send(
-        wgt, wbuf.at[y, pl.ds(pl.multiple_of(QTR * s_q, QTR), QTR)], w1a,
-        place(y, s_y, (z + 4 * step) % 16, s_c),
-    )
-    a_id = new_id()
-    send(act.at[:, pl.ds(pl.multiple_of(HALF * (1 - c), HALF), HALF)], a2.at[mine], a_id, c_dev)
 
     for d in (1, 3, 2):
         rows_d = pl.ds(pl.multiple_of(HD * ((y - d + 4) % 4), HD), HD)
@@ -162,127 +164,153 @@
         rows_d = pl.ds(pl.multiple_of(HD * ((y - n + 4) % 4), HD), HD)
         got(gt.at[rows_d, theirs], g_c + n)
 
-    def term(q, half):
+    halves = (slice(0, HALF // 2), slice(HALF // 2, HALF))
+
+    def term(q, p, half):
         return jnp.dot(
-            gt[pl.ds(pl.multiple_of(HD * q, HD), HD), :],
-            a2[:, HALF // 2 * half : HALF // 2 * (half + 1)],
+            gt[pl.ds(pl.multiple_of(HD * q + CH * p, CH), CH), :],
+            a2[:, halves[half]],
             preferred_element_type=F32,
         )
 
-    r1_id = new_id(6)
-    tt[0] = term(xo, 0).astype(BF16)
-    send(tt.at[0], r1.at[0], r1_id, xr_dev)
-    tt[1] = term(xo, 1).astype(BF16)
-    send(tt.at[1], r1.at[1], r1_id + 1, xl_dev)
-    tt[2] = term(xr, 1).astype(BF16)
-    send(tt.at[2], r1.at[2], r1_id + 2, xr_dev)
-    tt[3] = term(xl, 0).astype(BF16)
-    send(tt.at[3], r1.at[3], r1_id + 3, xl_dev)
-    tmg[0] = term(xr, 0)
-    tmg[1] = term(xl, 1)
+    r1_id = new_id(12)
+
+    def send_term(p, n, block, dev):
+        tt[p, n] = block.astype(BF16)
+        send(tt.at[p, n], r1.at[p, n], r1_id + 6 * p + n, dev)
+
+    for p in range(2):
+        send_term(p, 0, term(xo, p, 0), xr_dev)
+        send_term(p, 1, term(xo, p, 1), xl_dev)
+    for p in range(2):
+        send_term(p, 2, term(xr, p, 1), xr_dev)
+        send_term(p, 3, term(xl, p, 0), xl_dev)
+        tmg[p, 0] = term(xr, p, 0)
+        tmg[p, 1] = term(xl, p, 1)
+
+    side = 1 - 2 * (z % 2)
+    w1b = new_id(6)
+    for p in range(2):
+        mine_q = wbuf.at[x, own_q, p]
+        got(mine_q, w1a + p)
+        send(mine_q, mine_q, w1b + 3 * p, z_dev(2 * side))
+        send(mine_q, mine_q, w1b + 3 * p + 1, z_dev(1))
+        send(mine_q, mine_q, w1b + 3 * p + 2, z_dev(-1))
+
+    for p in range(2):
+        sx[p, :, halves[0]] = term(x, p, 0)
+        sx[p, :, halves[1]] = term(x, p, 1)
+    for p in range(2):
+        got(r1.at[p, 0], r1_id + 6 * p)
+        send_term(p, 4, tmg[p, 0] + r1[p, 0].astype(F32), xr_dev)
+        got(r1.at[p, 1], r1_id + 6 * p + 1)
+        send_term(p, 5, tmg[p, 1] + r1[p, 1].astype(F32), xl_dev)
+
+    w2 = new_id(12)
+    lo, hi = pl.ds(0, 2), pl.ds(2, 2)
+
+    def send_block(q, part, p, n, dev):
+        ref = wbuf.at[q, part, p]
+        send(ref, ref, w2 + 6 * p + n, dev)
+
+    for p in range(2):
+        got(wbuf.at[x, (z + 3) % 4, p], w1b + 3 * p + 1)
+        got(wbuf.at[x, (z + 1) % 4, p], w1b + 3 * p + 2)
+        got(wbuf.at[x, (z + 2) % 4, p], w1b + 3 * p)
+        send_block(x, lo, p, 0, xr_dev)
+        send_block(x, hi, p, 1, xl_dev)
+    for p in range(2):
+        send_block(x, hi, p, 2, xr_dev)
+        send_block(x, lo, p, 3, xl_dev)
 
     def quarter_of(q):
         return pl.ds(pl.multiple_of(QTR * (q % 4), QTR), QTR)
 
-    side = 1 - 2 * (z % 2)
-    mine_q = wbuf.at[x, quarter_of(own_q)]
-    got(mine_q, w1a)
-    w1b = new_id(3)
-    send(mine_q, mine_q, w1b, z_dev(2 * side))
-    send(mine_q, mine_q, w1b + 1, z_dev(1))
-    send(mine_q, mine_q, w1b + 2, z_dev(-1))
-
-    top, bot = slice(0, HALF // 2), slice(HALF // 2, HALF)
-    sx[:, top] = term(x, 0)
-    sx[:, bot] = term(x, 1)
-    got(r1.at[0], r1_id)
-    tt[4] = (tmg[0] + r1[0].astype(F32)).astype(BF16)
-    send(tt.at[4], r1.at[4], r1_id + 4, xr_dev)
-    got(r1.at[1], r1_id + 1)
-    tt[5] = (tmg[1] + r1[1].astype(F32)).astype(BF16)
-    send(tt.at[5], r1.at[5], r1_id + 5, xl_dev)
-
-    got(wbuf.at[x, quarter_of(z - 1 + 4)], w1b + 1)
-    got(wbuf.at[x, quarter_of(z + 1)], w1b + 2)
-    got(wbuf.at[x, quarter_of(z + 2)], w1b)
-    lo, hi = pl.ds(0, HALF // 2), pl.ds(HALF // 2, HALF // 2)
-    w2 = new_id(6)
-    send(wbuf.at[x, lo], wbuf.at[x, lo], w2, xr_dev)
-    send(wbuf.at[x, hi], wbuf.at[x, hi], w2 + 1, xl_dev)
-    send(wbuf.at[x, hi], wbuf.at[x, hi], w2 + 2, xr_dev)
-    send(wbuf.at[x, lo], wbuf.at[x, lo], w2 + 3, xl_dev)
+    z_id = new_id(6)
+    for p in range(2):
+        for n in (3, 2, 4, 5):
+            got(r1.at[p, n], r1_id + 6 * p + n)
+        sx[p, :, halves[0]] += r1[p, 3].astype(F32) + r1[p, 4].astype(F32)
+        sx[p, :, halves[1]] += r1[p, 2].astype(F32) + r1[p, 5].astype(F32)
+        for n, d in enumerate((-2 * side, 1, -1)):
+            zr[p, 3 + n] = sx[p, :, quarter_of(z + d + 16)].astype(BF16)
+            send(zr.at[p, 3 + n], zr.at[p, n], z_id + 3 * p + n, z_dev(d))
 
     v1 = new_id(4)
+    v2 = new_id(3)
 
     def values_of(q, n):
-        pp[q] = jnp.dot(a2[...], wbuf[q], preferred_element_type=F32)
+        pp[q] = jnp.dot(a2[...], wbuf[q].reshape(HALF, HD), preferred_element_type=F32)
         send(pp.at[q, theirs], pr.at[q], v1 + n, c_dev)
 
-    got(r1.at[3], r1_id + 3)
-    got(r1.at[2], r1_id + 2)
-    got(r1.at[4], r1_id + 4)
-    got(r1.at[5], r1_id + 5)
-    sx[:, top] = sx[:, top] + (r1[3].astype(F32) + r1[4].astype(F32))
-    sx[:, bot] = sx[:, bot] + (r1[2].astype(F32) + r1[5].astype(F32))
-    z_id = new_id(3)
-    for n, d in enumerate((-2 * side, 1, -1)):
-        zr[3 + n] = sx[:, quarter_of(z + d + 16)].astype(BF16)
-        send(zr.at[3 + n], zr.at[n], z_id + n, z_dev(d))
+    def values_out(q, n):
+        got(pr.at[q], v1 + n)
+        d = (q - y + 4) % 4
+
+        @pl.when(d != 0)
+        def _():
+            vs[d - 1] = (pp[q, mine] + pr[q]).astype(BF16)
+            pltpu.make_async_remote_copy(
+                src_ref=vs.at[d - 1], dst_ref=vr.at[d - 1], send_sem=ssem.at[v2 + d - 1],
+                recv_sem=rsem.at[v2 + d - 1], device_id=y_dev(d), device_id_type=MESH,
+            ).start()
 
     values_of(x, 0)
-    got(wbuf.at[xl, lo], w2)
-    send(wbuf.at[xl, lo], wbuf.at[xl, lo], w2 + 4, xr_dev)
-    got(wbuf.at[xr, hi], w2 + 1)
-    send(wbuf.at[xr, hi], wbuf.at[xr, hi], w2 + 5, xl_dev)
-
-    for n in range(3):
-        got(zr.at[n], z_id + n)
-    rb[...] = (
-        sx[:, quarter_of(own_q)]
-        + zr[0].astype(F32) + zr[1].astype(F32) + zr[2].astype(F32)
-    ).astype(BF16)
-    o_id = new_id(4)
-    for k in range(4):
-        src = rb.at[pl.ds(32 * k, 32)]
-        stay = jnp.logical_and(is_self, k == r)
-
-        @pl.when(jnp.logical_not(stay))
-        def _():
-            pltpu.make_async_remote_copy(
-                src_ref=src, dst_ref=ob.at[z // 4], send_sem=ssem.at[o_id + k],
-                recv_sem=rsem.at[o_id + z // 4], device_id=owner_dev(k), device_id_type=MESH,
-            ).start()
-
-        @pl.when(stay)
-        def _():
-            pltpu.make_async_copy(src, ob.at[z // 4], rsem.at[o_id + z // 4]).start()
-
-    got(wbuf.at[xl, hi], w2 + 2)
+    for p in range(2):
+        got(wbuf.at[xl, lo, p], w2 + 6 * p)
+        send_block(xl, lo, p, 4, xr_dev)
+        got(wbuf.at[xr, hi, p], w2 + 6 * p + 1)
+        send_block(xr, hi, p, 5, xl_dev)
+    values_out(x, 0)
+
+    o_id = new_id(8)
+    for p in range(2):
+        for n in range(3):
+            got(zr.at[p, n], z_id + 3 * p + n)
+        rb[p] = (
+            sx[p, :, quarter_of(own_q)]
+            + zr[p, 0].astype(F32) + zr[p, 1].astype(F32) + zr[p, 2].astype(F32)
+        ).astype(BF16)
+        for k in range(4):
+            src = rb.at[p, pl.ds(16 * k, 16)]
+            stay = jnp.logical_and(is_self, k == r)
+
+            @pl.when(jnp.logical_not(stay))
+            def _():
+                pltpu.make_async_remote_copy(
+                    src_ref=src, dst_ref=ob.at[z // 4, p], send_sem=ssem.at[o_id + 4 * p + k],
+                    recv_sem=rsem.at[o_id + 4 * p + z // 4], device_id=owner_dev(k),
+                    device_id_type=MESH,
+                ).start()
+
+            @pl.when(stay)
+            def _():
+                pltpu.make_async_copy(src, ob.at[z // 4, p], rsem.at[o_id + 4 * p + z // 4]).start()
+
+    for p in range(2):
+        got(wbuf.at[xl, hi, p], w2 + 6 * p + 2)
+        got(wbuf.at[xr, lo, p], w2 + 6 * p + 3)
     values_of(xl, 1)
-    got(wbuf.at[xr, lo], w2 + 3)
     values_of(xr, 2)
-    got(wbuf.at[xo, lo], w2 + 4)
-    got(wbuf.at[xo, hi], w2 + 5)
+    values_out(xl, 1)
+    values_out(xr, 2)
+    for p in range(2):
+        got(wbuf.at[xo, lo, p], w2 + 6 * p + 4)
+        got(wbuf.at[xo, hi, p], w2 + 6 * p + 5)
     values_of(xo, 3)
-
-    for n, q in ((0, x), (2, xl), (1, xr), (3, xo)):
-        got(pr.at[q], v1 + n)
-    v2 = new_id(3)
-    for d in (2, 1, 3):
-        q = (y + d) % 4
-        vs[d - 1] = (pp[q, mine] + pr[q]).astype(BF16)
-        send(vs.at[d - 1], vr.at[d - 1], v2 + d - 1, y_dev(d))
-
-    for k in range(4):
-        got(ob.at[k], o_id + k)
-    quarter = pl.ds(pl.multiple_of(32 * r, 32), 32)
-    gf[quarter, :] = (
+    values_out(xo, 3)
+
+    for p in range(2):
+        for k in range(4):
+            got(ob.at[k, p], o_id + 4 * p + k)
+    quarter = pl.ds(pl.multiple_of(16 * r, 16), 16)
+    gf[:, quarter, :] = (
         ob[0].astype(F32) + ob[1].astype(F32) + ob[2].astype(F32) + ob[3].astype(F32)
     ) * (1.0 / RANKS)
     f_id = new_id(3)
     for d in (1, 2, 3):
         rd = (r + d) % 4
-        send(gf.at[quarter], gf.at[quarter], f_id + d - 1, (y, s, rd))
+        send(gf.at[:, quarter], gf.at[:, quarter], f_id + d - 1, (y, s, rd))
 
     for d in (1, 2, 3):
         got(vr.at[d - 1], v2 + d - 1)
@@ -300,17 +328,19 @@
         gqv[:, lanes] = gq.T.astype(BF16)
         return acc + jnp.dot(gs, qv[:, lanes], preferred_element_type=F32)
 
-    gkv[...] = lax.fori_loop(0, HEADS, backward_head, jnp.zeros((TOK, HD), F32)).astype(BF16)
+    gkv[...] = lax.fori_loop(
+        0, HEADS, backward_head, jnp.zeros((TOK, HD), F32), unroll=2
+    ).astype(BF16)
     outs = [pltpu.make_async_copy(gqv, o_gq, lsem.at[8]), pltpu.make_async_copy(gkv, o_gk, lsem.at[9])]
     for cp in outs:
         cp.start()
 
     for d in (1, 2, 3):
-        other = pl.ds(pl.multiple_of(32 * ((r - d + 4) % 4), 32), 32)
-        got(gf.at[other], f_id + d - 1)
+        other = pl.ds(pl.multiple_of(16 * ((r - d + 4) % 4), 16), 16)
+        got(gf.at[:, other], f_id + d - 1)
     for cp in copies[5:]:
         cp.wait()
-    gradient = gf[...].T
+    gradient = gf[...].reshape(HD, QTR).T
     new_first = BETA_FIRST * fstv[...] + (1.0 - BETA_FIRST) * gradient
     new_second = BETA_SECOND * sndv[...] + (1.0 - BETA_SECOND) * gradient * gradient
     corrected = (
@@ -329,17 +359,43 @@
 
     for src, i in sends:
         pltpu.make_async_copy(src, src, ssem.at[i]).wait()
-    for k in range(4):
-        src = rb.at[pl.ds(32 * k, 32)]
-
-        @pl.when(jnp.logical_not(jnp.logical_and(is_self, k == r)))
-        def _():
-            pltpu.make_async_copy(src, src, ssem.at[o_id + k]).wait()
+    for d in (1, 2, 3):
+        pltpu.make_async_copy(vs.at[d - 1], vs.at[d - 1], ssem.at[v2 + d - 1]).wait()
+    for p in range(2):
+        for k in range(4):
+            src = rb.at[p, pl.ds(16 * k, 16)]
+
+            @pl.when(jnp.logical_not(jnp.logical_and(is_self, k == r)))
+            def _():
+                pltpu.make_async_copy(src, src, ssem.at[o_id + 4 * p + k]).wait()
     for cp in outs:
         cp.wait()
 
 
-N_SEM = 48
+def hand_over(*refs):
+    src, dst, held, sem = refs[:6], refs[6:12], refs[12:18], refs[18]
+    moves = []
+    for n in range(6):
+        rows = src[n].shape[0] // (4 if n == 0 else 1)
+        moves += [(n, pl.ds(rows * k, rows)) for k in range(4 if n == 0 else 1)]
+    into = [
+        pltpu.make_async_copy(src[n].at[rows], held[n].at[rows], sem.at[0, i])
+        for i, (n, rows) in enumerate(moves)
+    ]
+    out = [
+        pltpu.make_async_copy(held[n].at[rows], dst[n].at[rows], sem.at[1, i])
+        for i, (n, rows) in enumerate(moves)
+    ]
+    for cp in into:
+        cp.start()
+    for cp, after in zip(into, out):
+        cp.wait()
+        after.start()
+    for cp in out:
+        cp.wait()
+
+
+N_SEM = 64
 
 
 def per_device(act, que, key, gout, seg, wgt, mas, fst, snd):
@@ -347,7 +403,7 @@
     any_spec = pl.BlockSpec(memory_space=pl.ANY)
     vm = pltpu.VMEM
     shard = (QTR, HD)
-    return pl.pallas_call(
+    results = pl.pallas_call(
         kernel,
         out_shape=(
             sds((TOK, HALF), BF16), sds((TOK, HD), BF16),
@@ -359,19 +415,19 @@
             vm((2 * TOK, HALF), BF16),
             vm((TOK, HEADS * HD), BF16), vm((TOK, HD), BF16), vm((TOK, HEADS * HD), BF16),
             vm((1, TOK), jnp.int32), vm(shard, F32), vm(shard, F32), vm(shard, F32),
-            vm((4, HALF, HD), BF16),
+            vm((4, 4, 2, HD, HD), BF16),
             vm((TOK, TOK), F32),
             vm((HEADS, TOK, TOK), F32),
             vm((TOK, HD), F32),
             vm((4 * HD, 2 * TOK), BF16),
-            vm((6, HD, HALF // 2), BF16),
-            vm((2, HD, HALF // 2), F32),
-            vm((6, HD, HALF // 2), BF16),
-            vm((HD, HALF), F32),
-            vm((6, HD, QTR), BF16),
-            vm((HD, QTR), BF16),
-            vm((4, 32, QTR), BF16),
-            vm((HD, QTR), F32),
+            vm((2, 6, CH, HALF // 2), BF16),
+            vm((2, 2, CH, HALF // 2), F32),
+            vm((2, 6, CH, HALF // 2), BF16),
+            vm((2, CH, HALF), F32),
+            vm((2, 6, CH, QTR), BF16),
+            vm((2, CH, QTR), BF16),
+            vm((4, 2, 16, QTR), BF16),
+            vm((2, CH, QTR), F32),
             vm((4, 2 * TOK, HD), F32),
             vm((4, TOK, HD), F32),
             vm((3, TOK, HD), BF16),
@@ -389,6 +445,14 @@
             collective_id=0, has_side_effects=True, vmem_limit_bytes=60 << 20
         ),
     )(act, que, key, gout, seg.reshape(1, TOK), wgt, mas, fst, snd)
+    return pl.pallas_call(
+        hand_over,
+        out_shape=tuple(sds(v.shape, v.dtype) for v in results),
+        in_specs=[any_spec] * 6,
+        out_specs=[any_spec] * 6,
+        scratch_shapes=[vm(v.shape, v.dtype) for v in results] + [pltpu.SemaphoreType.DMA((2, 9))],
+        compiler_params=pltpu.CompilerParams(vmem_limit_bytes=60 << 20),
+    )(*results)
 
 
 def solution(mesh):

time: 65.8 us -> 60.7 us (0.922)
  the two profiles are of different devices: /device:TPU:1 before, /device:TPU:4 now
where the time goes in v3:
time: 60.7 us; the launch traced here: 60.5 us
  Pallas kernels  59.9 us (99%)
  between operations  0.64 us (1%)
    pallas_call x1, Pallas kernels, per_device(): pl.pallas_call(kernel, out_shape=(sds((TOK, HALF), BF16), sds((TOK, HD),...  57.8 us
    pallas_call x1, Pallas kernels, per_device(): pl.pallas_call(hand_over, out_shape=tuple((sds(v.shape, v.dtype) for v in...  2.13 us

profile of v3, /device:TPU:4, one launch (start us, length us, event | category | flops | bytes accessed | tf_op | source)
XLA Modules:
  0.0 60.5 jit_solution(2138407200012827020)
XLA Ops:
  0.6 57.8 %shard_map.136 = (bf16[256,1024]{1,0:T(8,128)(2,1)}, bf16[256,128]{1,0:T(8,128)(2,1)}, f32[256,128]{1,0:T(8,128)}, f32[256,128]{1,0:T(8,128)}, f32[256,128]{1,0:T(8,128)}, /*index=5*/f32[256,128]{1,0:T(8,128)}) custom-call(bf16[256,2048]{1,0:T(8,128)(2,1)} %act.1, bf16[256,1024]{1,0:T(8,128)(2,1)} %que.1, bf16[256,128]{1,0:T(8,128)(2,1)} %key.1, ...), custom_call_target="tpu_custom_call" | custom-call | tf_op jit(solution)/shard_map/pallas_call | solution.py:406
  58.4 2.1 %shard_map.137 = (bf16[256,1024]{1,0:T(8,128)(2,1)}, bf16[256,128]{1,0:T(8,128)(2,1)}, f32[256,128]{1,0:T(8,128)}, f32[256,128]{1,0:T(8,128)}, f32[256,128]{1,0:T(8,128)}, /*index=5*/f32[256,128]{1,0:T(8,128)}) custom-call(bf16[256,1024]{1,0:T(8,128)(2,1)} %get-tuple-element.12.refs_0_, bf16[256,128]{1,0:T(8,128)(2,1)} %get-tuple-element.13.refs_1_, ...), custom_call_target="tpu_custom_call" | custom-call | tf_op jit(solution)/shard_map/pallas_call | solution.py:448

commit v4 on v3

--- a/solution.py
+++ b/solution.py
@@ -78,16 +78,14 @@
         return place(x, y, (z + d + 16) % 16, c)
 
     s_y, s_c, s_q = s // 8, (s % 8) // 4, s % 4
-    own_q = z % 4
+    own_q = (z + 2) % 4
     own_s, own_y = 8 * y + 4 * c + own_q, x
 
     def rep_dev(k):
-        return place(y, s_y, 4 * k + s_q, s_c)
+        return place(y, s_y, 4 * k + (s_q + 2) % 4, s_c)
 
     def owner_dev(k):
         return (own_y, own_s, k)
-
-    is_self = jnp.logical_and(own_s == s, own_y == y)
 
     barrier = pltpu.get_barrier_semaphore()
     for dev in [c_dev, xr_dev, xl_dev, place(x + 1 - 2 * (x % 2), y, z, 1 - c)] + [
@@ -95,13 +93,8 @@
     ] + [z_dev(d) for d in (-2, -1, 1, 2)]:
         pl.semaphore_signal(barrier, inc=1, device_id=dev, device_id_type=MESH)
     for k in range(4):
-        @pl.when(jnp.logical_not(jnp.logical_and(is_self, k == r)))
-        def _():
-            pl.semaphore_signal(barrier, inc=1, device_id=owner_dev(k), device_id_type=MESH)
-
-        @pl.when(jnp.logical_not(jnp.logical_and(is_self, k == z // 4)))
-        def _():
-            pl.semaphore_signal(barrier, inc=1, device_id=rep_dev(k), device_id_type=MESH)
+        pl.semaphore_signal(barrier, inc=1, device_id=owner_dev(k), device_id_type=MESH)
+        pl.semaphore_signal(barrier, inc=1, device_id=rep_dev(k), device_id_type=MESH)
 
     mine = pl.ds(pl.multiple_of(TOK * c, TOK), TOK)
     theirs = pl.ds(pl.multiple_of(TOK * (1 - c), TOK), TOK)
@@ -133,14 +126,13 @@
         return acc + jnp.dot(weights.astype(BF16), gov[:, lanes], preferred_element_type=F32)
 
     acc = lax.fori_loop(0, 6, forward_head, jnp.zeros((TOK, HD), F32), unroll=2)
-    pl.semaphore_wait(barrier, 19 - 2 * is_self.astype(jnp.int32))
+    pl.semaphore_wait(barrier, 19)
 
     w1a = new_id(2)
-    step = (r - 2 * (y % 2) - s_c + 9) % 4
     for p in range(2):
         send(
             wgt.at[pl.ds(HD * p, HD)], wbuf.at[y, s_q, p], w1a + p,
-            place(y, s_y, (z + 4 * step) % 16, s_c),
+            place(y, s_y, (z + 2 + 4 * r) % 16, s_c),
         )
     a_id = new_id()
     send(act.at[:, pl.ds(pl.multiple_of(HALF * (1 - c), HALF), HALF)], a2.at[mine], a_id, c_dev)
@@ -214,9 +206,9 @@
         send(ref, ref, w2 + 6 * p + n, dev)
 
     for p in range(2):
-        got(wbuf.at[x, (z + 3) % 4, p], w1b + 3 * p + 1)
-        got(wbuf.at[x, (z + 1) % 4, p], w1b + 3 * p + 2)
-        got(wbuf.at[x, (z + 2) % 4, p], w1b + 3 * p)
+        got(wbuf.at[x, (z + 1) % 4, p], w1b + 3 * p + 1)
+        got(wbuf.at[x, (z + 3) % 4, p], w1b + 3 * p + 2)
+        got(wbuf.at[x, z % 4, p], w1b + 3 * p)
         send_block(x, lo, p, 0, xr_dev)
         send_block(x, hi, p, 1, xl_dev)
     for p in range(2):
@@ -233,7 +225,7 @@
         sx[p, :, halves[0]] += r1[p, 3].astype(F32) + r1[p, 4].astype(F32)
         sx[p, :, halves[1]] += r1[p, 2].astype(F32) + r1[p, 5].astype(F32)
         for n, d in enumerate((-2 * side, 1, -1)):
-            zr[p, 3 + n] = sx[p, :, quarter_of(z + d + 16)].astype(BF16)
+            zr[p, 3 + n] = sx[p, :, quarter_of(z + d + 18)].astype(BF16)
             send(zr.at[p, 3 + n], zr.at[p, n], z_id + 3 * p + n, z_dev(d))
 
     v1 = new_id(4)
@@ -256,15 +248,12 @@
             ).start()
 
     values_of(x, 0)
+    o_id = new_id(8)
     for p in range(2):
         got(wbuf.at[xl, lo, p], w2 + 6 * p)
         send_block(xl, lo, p, 4, xr_dev)
         got(wbuf.at[xr, hi, p], w2 + 6 * p + 1)
         send_block(xr, hi, p, 5, xl_dev)
-    values_out(x, 0)
-
-    o_id = new_id(8)
-    for p in range(2):
         for n in range(3):
             got(zr.at[p, n], z_id + 3 * p + n)
         rb[p] = (
@@ -272,21 +261,13 @@
             + zr[p, 0].astype(F32) + zr[p, 1].astype(F32) + zr[p, 2].astype(F32)
         ).astype(BF16)
         for k in range(4):
-            src = rb.at[p, pl.ds(16 * k, 16)]
-            stay = jnp.logical_and(is_self, k == r)
-
-            @pl.when(jnp.logical_not(stay))
-            def _():
-                pltpu.make_async_remote_copy(
-                    src_ref=src, dst_ref=ob.at[z // 4, p], send_sem=ssem.at[o_id + 4 * p + k],
-                    recv_sem=rsem.at[o_id + 4 * p + z // 4], device_id=owner_dev(k),
-                    device_id_type=MESH,
-                ).start()
-
-            @pl.when(stay)
-            def _():
-                pltpu.make_async_copy(src, ob.at[z // 4, p], rsem.at[o_id + 4 * p + z // 4]).start()
-
+            pltpu.make_async_remote_copy(
+                src_ref=rb.at[p, pl.ds(16 * k, 16)], dst_ref=ob.at[z // 4, p],
+                send_sem=ssem.at[o_id + 4 * p + k], recv_sem=rsem.at[o_id + 4 * p + z // 4],
+                device_id=owner_dev(k), device_id_type=MESH,
+            ).start()
+
+    values_out(x, 0)
     for p in range(2):
         got(wbuf.at[xl, hi, p], w2 + 6 * p + 2)
         got(wbuf.at[xr, lo, p], w2 + 6 * p + 3)
@@ -364,10 +345,7 @@
     for p in range(2):
         for k in range(4):
             src = rb.at[p, pl.ds(16 * k, 16)]
-
-            @pl.when(jnp.logical_not(jnp.logical_and(is_self, k == r)))
-            def _():
-                pltpu.make_async_copy(src, src, ssem.at[o_id + 4 * p + k]).wait()
+            pltpu.make_async_copy(src, src, ssem.at[o_id + 4 * p + k]).wait()
     for cp in outs:
         cp.wait()
 

time: 60.7 us -> 59.2 us (0.975)
  Pallas kernels: 59.9 us -> 58.4 us
    pallas_call x1, Pallas kernels: 57.8 us -> 56.3 us  [per_device(): pl.pallas_call(kernel, out_shape=(sds((TOK, HALF), BF16), sds((TOK, HD),...]
where the time goes in v4:
time: 59.2 us; the launch traced here: 59.1 us
  Pallas kernels  58.4 us (99%)
  between operations  0.64 us (1%)
    pallas_call x1, Pallas kernels, per_device(): pl.pallas_call(kernel, out_shape=(sds((TOK, HALF), BF16), sds((TOK, HD),...  56.3 us
    pallas_call x1, Pallas kernels, per_device(): pl.pallas_call(hand_over, out_shape=tuple((sds(v.shape, v.dtype) for v in...  2.13 us

profile of v4, /device:TPU:4, one launch (start us, length us, event | category | flops | bytes accessed | tf_op | source)
XLA Modules:
  0.0 59.1 jit_solution(14875313048427828354)
XLA Ops:
  0.6 56.3 %shard_map.136 = (bf16[256,1024]{1,0:T(8,128)(2,1)}, bf16[256,128]{1,0:T(8,128)(2,1)}, f32[256,128]{1,0:T(8,128)}, f32[256,128]{1,0:T(8,128)}, f32[256,128]{1,0:T(8,128)}, /*index=5*/f32[256,128]{1,0:T(8,128)}) custom-call(bf16[256,2048]{1,0:T(8,128)(2,1)} %act.1, bf16[256,1024]{1,0:T(8,128)(2,1)} %que.1, bf16[256,128]{1,0:T(8,128)(2,1)} %key.1, ...), custom_call_target="tpu_custom_call" | custom-call | tf_op jit(solution)/shard_map/pallas_call | solution.py:384
  56.9 2.1 %shard_map.137 = (bf16[256,1024]{1,0:T(8,128)(2,1)}, bf16[256,128]{1,0:T(8,128)(2,1)}, f32[256,128]{1,0:T(8,128)}, f32[256,128]{1,0:T(8,128)}, f32[256,128]{1,0:T(8,128)}, /*index=5*/f32[256,128]{1,0:T(8,128)}) custom-call(bf16[256,1024]{1,0:T(8,128)(2,1)} %get-tuple-element.12.refs_0_, bf16[256,128]{1,0:T(8,128)(2,1)} %get-tuple-element.13.refs_1_, ...), custom_call_target="tpu_custom_call" | custom-call | tf_op jit(solution)/shard_map/pallas_call | solution.py:426

commit v5 on v4

--- a/solution.py
+++ b/solution.py
@@ -125,7 +125,7 @@
         wst[h] = weights
         return acc + jnp.dot(weights.astype(BF16), gov[:, lanes], preferred_element_type=F32)
 
-    acc = lax.fori_loop(0, 6, forward_head, jnp.zeros((TOK, HD), F32), unroll=2)
+    acc = lax.fori_loop(0, HEADS, forward_head, jnp.zeros((TOK, HD), F32), unroll=2)
     pl.semaphore_wait(barrier, 19)
 
     w1a = new_id(2)
@@ -137,7 +137,6 @@
     a_id = new_id()
     send(act.at[:, pl.ds(pl.multiple_of(HALF * (1 - c), HALF), HALF)], a2.at[mine], a_id, c_dev)
 
-    acc = lax.fori_loop(6, HEADS, forward_head, acc, unroll=2)
     gyt = pl.ds(pl.multiple_of(HD * y, HD), HD)
     gt[gyt, mine] = acc.T.astype(BF16)
     g_y = new_id(3)

time: 59.2 us -> 57.9 us (0.978)
  the two profiles are of different devices: /device:TPU:4 before, /device:TPU:1 now
where the time goes in v5:
time: 57.9 us; the launch traced here: 56.9 us
  Pallas kernels  56.3 us (97%)
  between operations  0.64 us (1%)
    pallas_call x1, Pallas kernels, per_device(): pl.pallas_call(kernel, out_shape=(sds((TOK, HALF), BF16), sds((TOK, HD),...  54.2 us
    pallas_call x1, Pallas kernels, per_device(): pl.pallas_call(hand_over, out_shape=tuple((sds(v.shape, v.dtype) for v in...  2.13 us

profile of v5, /device:TPU:1, one launch (start us, length us, event | category | flops | bytes accessed | tf_op | source)
XLA Modules:
  0.0 56.9 jit_solution(10474967693555031559)
XLA Ops:
  0.6 54.2 %shard_map.136 = (bf16[256,1024]{1,0:T(8,128)(2,1)}, bf16[256,128]{1,0:T(8,128)(2,1)}, f32[256,128]{1,0:T(8,128)}, f32[256,128]{1,0:T(8,128)}, f32[256,128]{1,0:T(8,128)}, /*index=5*/f32[256,128]{1,0:T(8,128)}) custom-call(bf16[256,2048]{1,0:T(8,128)(2,1)} %act.1, bf16[256,1024]{1,0:T(8,128)(2,1)} %que.1, bf16[256,128]{1,0:T(8,128)(2,1)} %key.1, ...), custom_call_target="tpu_custom_call" | custom-call | tf_op jit(solution)/shard_map/pallas_call | solution.py:383
  54.8 2.1 %shard_map.137 = (bf16[256,1024]{1,0:T(8,128)(2,1)}, bf16[256,128]{1,0:T(8,128)(2,1)}, f32[256,128]{1,0:T(8,128)}, f32[256,128]{1,0:T(8,128)}, f32[256,128]{1,0:T(8,128)}, /*index=5*/f32[256,128]{1,0:T(8,128)}) custom-call(bf16[256,1024]{1,0:T(8,128)(2,1)} %get-tuple-element.12.refs_0_, bf16[256,128]{1,0:T(8,128)(2,1)} %get-tuple-element.13.refs_1_, ...), custom_call_target="tpu_custom_call" | custom-call | tf_op jit(solution)/shard_map/pallas_call | solution.py:425
